TPU v7x, 128 devices: a whole 4x4x4 slice. The times are simulated.
128 devices in a mesh: dp: 8 (over x, core), seq: 16 (over z, y).
Axes of the slice: x: 4, y: 4, z: 4, core: 2. Of those that a mesh axis runs over, the one named last changes fastest.
Arguments:
- trunk: bfloat16 [8, 4096, 1536], P('dp', 'seq'), may hold values from -34 to 34
- skip: bfloat16 [8, 8192, 1536], P('dp', 'seq'), may hold values from -6 to 6
- valid_bins: int32 [8], P('dp'), may hold values from 2048 to 4096, as said below
- query_weight: bfloat16 [1536, 256], replicated
- key_weight: bfloat16 [1536, 256], replicated
- value_weight: bfloat16 [1536, 768], replicated, may hold values from -0.15625 to 0.15625
- out_weight: bfloat16 [768, 1536], replicated, may hold values from -0.21875 to 0.21875
- depth_weight: float32 [3, 1536], replicated, may hold values from -3 to 3
- point_weight: bfloat16 [1536, 1536], replicated, may hold values from -0.15625 to 0.15625
- cotangent: bfloat16 [8, 8192, 1536], P('dp', 'seq'), may hold values from -6 to 6
Outputs:
- grad_pointwise: bfloat16 [1536, 1536], replicated
- grad_depthwise: float32 [3, 1536], replicated
- grad_skip: bfloat16 [8, 8192, 1536], P('dp', 'seq')
Inputs may be any that keep to these rules, and one draw needn't show every extreme that they name: Bins at or past a window's valid_bins are padding; in every draw some window is whole.
All inputs are finite; a program needn't handle non-finite values.
Results may differ from a plain program's by a relative error of at most 0.017.
Values may be sent and summed in bfloat16 or wider, within the bound.
No kernel may reach another device: no remote copies, remote signals or barrier semaphores. Data moves between devices by JAX's collectives and lax.ppermute only.
A program may use at most 128 MiB of HBM per device.

v0:
```python
from functools import partial
import math
import jax
import jax.numpy as jnp
from jax import lax
from jax.sharding import PartitionSpec as P

H = 4
DH = 64
DV = 192


def padded_2(cells, sides, width):
    for axis, dim in sides:
        count = lax.axis_size(axis)
        ends = count - 1
        head = lax.slice_in_dim(cells, 0, width, axis=dim)
        tail = lax.slice_in_dim(cells, cells.shape[dim] - width, cells.shape[dim], axis=dim)
        cells = jnp.concatenate(
            [
                lax.ppermute(tail, axis, [(i, (i + 1) % count) for i in range(ends)]),
                cells,
                lax.ppermute(head, axis, [((i + 1) % count, i) for i in range(ends)]),
            ],
            axis=dim,
        )
    return cells


def local(
    trunk,
    skip,
    valid_bins,
    query_weight,
    key_weight,
    value_weight,
    out_weight,
    depth_weight,
    point_weight,
    cotangent,
):
    tokens = trunk[0]
    row_count = tokens.shape[0]
    score_scale = 1.0 / math.sqrt(DH)
    queries = (
        jnp.dot(tokens, query_weight, preferred_element_type=jnp.float32)
        .astype(jnp.bfloat16)
        .reshape(row_count, H, DH)
    )
    keys = jnp.dot(tokens, key_weight, preferred_element_type=jnp.float32).astype(jnp.bfloat16)
    values = jnp.dot(tokens, value_weight, preferred_element_type=jnp.float32).astype(jnp.bfloat16)
    limit = valid_bins[0]
    running_max = jnp.full((H, row_count), -1e30, jnp.float32)
    weighted = jnp.zeros((row_count, H, DV), jnp.float32)
    key_piece = lax.all_gather(keys, "seq", axis=0, tiled=True)
    value_piece = lax.all_gather(values, "seq", axis=0, tiled=True)
    width = key_piece.shape[0]
    key_heads = key_piece.reshape(width, H, DH)
    value_heads = value_piece.reshape(width, H, DV)
    scores = (
        jnp.einsum("qhd,khd->hqk", queries, key_heads, preferred_element_type=jnp.float32)
        * score_scale
    )
    places = jnp.arange(width, dtype=jnp.int32)
    scores = jnp.where(places[None, None, :] < limit, scores, -1e30)
    fresh_max = jnp.maximum(running_max, jnp.max(scores, axis=2))
    shrink = jnp.exp(running_max - fresh_max)
    weights_raw = jnp.exp(scores - fresh_max[:, :, None])
    running_total = jnp.sum(weights_raw, axis=2)
    update = jnp.einsum(
        "hqk,khd->qhd",
        weights_raw.astype(jnp.bfloat16),
        value_heads,
        preferred_element_type=jnp.float32,
    )
    weighted = weighted * shrink.T[:, :, None] + update
    running_max, running_total, weighted = (fresh_max, running_total, weighted)
    mixed = (weighted / running_total.T[:, :, None]).reshape(row_count, H * DV)
    attended = (mixed * lax.rsqrt(jnp.mean(mixed * mixed, axis=1, keepdims=True) + 1e-05)).astype(
        jnp.bfloat16
    )
    hidden = (
        tokens.astype(jnp.float32)
        + jnp.dot(attended, out_weight, preferred_element_type=jnp.float32)
    ).astype(jnp.bfloat16)
    upsampled = (
        jnp.repeat(hidden, 2, axis=0).astype(jnp.float32) + skip[0].astype(jnp.float32)
    ).astype(jnp.bfloat16)
    padded = padded_2(upsampled, (("seq", 0),), 1)
    pre_act = (
        depth_weight[0] * padded[:-2]
        + depth_weight[1] * padded[1:-1]
        + depth_weight[2] * padded[2:]
    )
    act_value, pullback = jax.vjp(partial(jax.nn.gelu, approximate=True), pre_act)
    activated = act_value.astype(jnp.bfloat16)
    upstream = cotangent[0]
    grad_act = lax.dot_general(
        upstream, point_weight, (((1,), (1,)), ((), ())), preferred_element_type=jnp.float32
    )
    grad_pre = pullback(grad_act)[0].astype(jnp.bfloat16)
    fine_rows = grad_pre.shape[0]
    grad_wide = grad_pre.astype(jnp.float32)
    depth_term = jnp.stack(
        [
            jnp.sum(padded[offset : offset + fine_rows].astype(jnp.float32) * grad_wide, axis=0)
            for offset in range(3)
        ]
    )
    grad_padded = padded_2(grad_pre, (("seq", 0),), 1)
    grad_skip = (
        depth_weight[0] * grad_padded[2:]
        + depth_weight[1] * grad_padded[1:-1]
        + depth_weight[2] * grad_padded[:-2]
    ).astype(jnp.bfloat16)
    norm_scale = 1.0 / math.sqrt(lax.axis_size("dp") * lax.axis_size("seq") * fine_rows)
    point_term = lax.dot_general(
        activated, upstream, (((0,), (0,)), ((), ())), preferred_element_type=jnp.float32
    )
    point_total, depth_total = lax.psum((point_term, depth_term), ("dp", "seq"))
    grad_pointwise = (point_total * norm_scale).astype(jnp.bfloat16)
    return (grad_pointwise, depth_total * norm_scale, grad_skip[None])


def solution(mesh):
    return jax.shard_map(
        local,
        mesh=mesh,
        in_specs=(
            P("dp", "seq", None),
            P("dp", "seq", None),
            P("dp"),
            P(),
            P(),
            P(),
            P(),
            P(),
            P(),
            P("dp", "seq", None),
        ),
        out_specs=(P(), P(), P("dp", "seq", None)),
        check_vma=False,
    )
```

profile of v0, /device:TPU:1, one launch (start us, length us, event | category | flops | bytes accessed | tf_op | source)
XLA Modules:
  0.0 349.5 jit_solution(12524377417579679030)
XLA Ops:
  7.2 0.0 copy-start
  7.2 0.0 copy-start.3
  7.2 0.0 all-gather.3.cloned.1.call-start
  7.2 2.6 convolution_convert_fusion.1
  9.8 0.0 all-gather.3.cloned.1.call-update
  9.8 0.0 all-gather.5.cloned.1.call-start
  9.9 3.4 convolution_convert_fusion
  13.3 0.0 all-gather.5.cloned.1.call-update
  13.4 0.0 all-reduce.2.cloned.1.call-start
  14.1 0.0 copy-done.3
  14.1 1.6 convolution_convert_fusion.2
  15.7 42.6 %all-gather.3.cloned.1.call-done = bf16[4096,256]{1,0:T(8,128)(2,1)} async-done(((bf16[256,256]{1,0:T(8,128)(2,1)}), bf16[4096,256]{1,0:T(8,128)(2,1)}) %all-gather.3.cloned.1.call-update) | async-done | bytes 2097168 | tf_op jit(solution)/shard_map/all_gather | solution.py:55
  58.2 4.1 %copy.15 = bf16[4096,256]{0,1:T(8,128)(2,1)} copy(bf16[4096,256]{1,0:T(8,128)(2,1)} %all-gather.3.cloned.1.call-done) | data formatting | bytes 4194304 | tf_op jit(solution)/shard_map/all_gather | solution.py:55
  62.3 4.1 %fusion = (f32[4,256]{1,0:T(4,128)S(1)}, f32[4,256,4096]{2,1,0:T(8,128)S(1)}) fusion(pred[4096]{0:T(1024)(128)(4,1)S(1)} %iota_compare_fusion, bf16[256,4,64]{0,2,1:T(8,128)(2,1)S(1)} %bitcast.49, bf16[4096,4,64]{0,2,1:T(8,128)(2,1)} %bitcast.47), kind=kOutput, calls=%fused_computation.2 | convolution fusion | flops 549452800 | bytes 19013632 | tf_op jit(solution)/shard_map/qhd,khd->hqk/dot_general | solution.py:61
  66.4 0.0 copy-start.2
  66.4 5.9 %copy-done.2 = f32[4,256,4096]{2,1,0:T(8,128)} copy-done((f32[4,256,4096]{2,1,0:T(8,128)}, f32[4,256,4096]{2,1,0:T(8,128)S(1)}, u32[]{:S(2)}) %copy-start.2) | copy-done | bytes 16777240
  72.4 4.0 %fusion.1 = f32[4,256]{1,0:T(4,128)S(1)} fusion(f32[4,256,4096]{2,1,0:T(8,128)S(1)} %get-tuple-element.17, f32[4,256]{1,0:T(4,128)S(1)} %get-tuple-element.15, pred[4096]{0:T(1024)(128)(4,1)S(1)} %iota_compare_fusion), kind=kLoop, calls=%fused_computation.3 | loop fusion | flops 16776192 | bytes 16789504 | tf_op jit(solution)/shard_map/reduce_sum | solution.py:69
  76.4 46.3 %all-gather.5.cloned.1.call-done = bf16[4096,768]{1,0:T(8,128)(2,1)} async-done(((bf16[256,768]{1,0:T(8,128)(2,1)}), bf16[4096,768]{1,0:T(8,128)(2,1)}) %all-gather.5.cloned.1.call-update) | async-done | bytes 6291472 | tf_op jit(solution)/shard_map/all_gather | solution.py:56
  122.7 8.6 %copy.16 = bf16[4096,768]{0,1:T(8,128)(2,1)} copy(bf16[4096,768]{1,0:T(8,128)(2,1)} %all-gather.5.cloned.1.call-done) | data formatting | bytes 12582912 | tf_op jit(solution)/shard_map/all_gather | solution.py:56
  131.3 10.3 %multiply_reduce_fusion = (f32[256]{0:T(256)S(1)}, f32[256,4,192]{0,2,1:T(8,128)S(1)}) fusion(f32[256,4]{0,1:T(4,128)S(1)} %bitcast.50, bf16[4096,4,192]{0,2,1:T(8,128)(2,1)} %bitcast.48, f32[4,256,4096]{2,1,0:T(8,128)} %copy-done.2, f32[4,256]{1,0:T(4,128)S(1)} %get-tuple-element.15, pred[4096]{0:T(1024)(128)(4,1)S(1)} %iota_compare_fusion, ...), kind=kOutput, calls=%fused_computation.68 | convolution fusion | flops 1628176128 | bytes 23872512 | tf_op jit(solution)/shard_map/hqk,khd->qhd/dot_general | solution.py:70
  141.6 0.1 fusion.51
  141.7 0.0 copy-done
  141.7 0.8 fusion.26
  142.5 2.7 broadcast_in_dim.33
  145.2 5.2 %convert_element_type.79 = f32[512,1536]{1,0:T(8,128)} reshape(f32[256,2,1536]{2,1,0:T(2,128)} %broadcast_in_dim.33) | data formatting | bytes 6291456 | tf_op jit(solution)/shard_map/convert_element_type | solution.py:87
  150.5 0.0 copy-start.4
  150.5 0.0 copy-start.5
  150.5 2.9 fusion.24
  153.4 3.1 collective-permute-start
  156.6 1.5 collective-permute-start.1
  158.0 0.0 copy-done.4
  158.0 0.1 slice_reduce_fusion.2
  158.1 0.0 collective-permute-done
  158.1 2.8 collective-permute-done.1
  160.9 0.0 copy-done.5
  160.9 6.6 %fusion.27 = f32[1536,1536]{1,0:T(8,128)} fusion(bf16[512,1536]{1,0:T(8,128)(2,1)S(1)} %fusion.24, bf16[1,1536]{1,0:T(2,128)(2,1)S(1)} %collective-permute-done.1, bf16[1,1536]{1,0:T(2,128)(2,1)S(1)} %collective-permute-done, bf16[1,512,1536]{2,1,0:T(8,128)(2,1)S(1)} %copy-done.5, f32[1536]{0:T(1024)S(1)} %get-tuple-element.7, ...), kind=kOutput, calls=%fused_computation.41 | convolution fusion | flops 2434007040 | bytes 12607488 | tf_op jit(solution)/shard_map/dot_general | solution.py:117
  167.5 0.0 all-reduce.2.cloned.1.call-update
  167.5 7.5 %fusion.17 = bf16[512,1536]{1,0:T(8,128)(2,1)S(1)} fusion(bf16[1,1536]{1,0:T(2,128)(2,1)S(1)} %collective-permute-done.1, bf16[512,1536]{1,0:T(8,128)(2,1)S(1)} %fusion.24, bf16[1,1536]{1,0:T(2,128)(2,1)S(1)} %collective-permute-done, bf16[1536,1536]{1,0:T(8,128)(2,1)} %param.18, bf16[1,512,1536]{2,1,0:T(8,128)(2,1)} %param.19, ...), kind=kOutput, calls=%fused_computation.28 | convolution fusion | flops 2442657792 | bytes 9461760 | tf_op jit(solution)/shard_map/dot_general | solution.py:98
  175.1 1.3 collective-permute-start.2
  176.4 4.0 %collective-permute-start.3 = (bf16[1,1536]{1,0:T(2,128)(2,1)S(1)}, bf16[1,1536]{1,0:T(2,128)(2,1)S(1)}, u32[]{:S(2)}, u32[]{:S(2)}) collective-permute-start(bf16[1,1536]{1,0:T(2,128)(2,1)S(1)} %get-tuple-element.11), channel_id=1, source_target_pairs={{0,1},{1,2},{2,3},{3,4},{4,5},{5,6},{6,7},{7,8},{8,9},{9,10},{10,1... | collective-permute-start | bytes 9224 | tf_op jit(solution)/shard_map/ppermute | solution.py:21
  180.4 0.0 collective-permute-done.2
  180.4 0.7 collective-permute-done.3
  181.1 3.5 %fusion.18 = (f32[1536]{0:T(1024)S(1)}, f32[1536]{0:T(1024)S(1)}, f32[1536]{0:T(1024)S(1)}, bf16[1,512,1536]{2,1,0:T(8,128)(2,1)}) fusion(bf16[512,1536]{1,0:T(8,128)(2,1)S(1)} %fusion.17, bf16[512,1536]{1,0:T(8,128)(2,1)S(1)} %fusion.24, bf16[1,1536]{1,0:T(2,128)(2,1)S(1)} %collective-permute-done, bf16[1,1536]{1,0:T(2,128)(2,1)S(1)} %collective-permute-done.1, ...), kind=kLoop, calls=%fused_computation.29 | loop fusion | flops 23588352 | bytes 4767744 | tf_op jit(solution)/shard_map/reduce_sum | solution.py:106
  184.7 74.9 %psum.15 = f32[3,1536]{1,0:T(4,128)S(1)} all-reduce(f32[3,1536]{1,0:T(4,128)S(1)} %pad_maximum_fusion.5), channel_id=1, replica_groups=mesh['dp'=8,'seq'=16] {'dp','seq'}, use_global_device_ids=true, to_apply=%region_7.8 | all-reduce | flops 4608 | bytes 36864 | tf_op jit(solution)/shard_map/psum | solution.py:120
  259.6 0.6 broadcast_multiply_fusion
  260.2 75.5 %all-reduce.2.cloned.1.call-done = f32[1536,1536]{1,0:T(8,128)} async-done(((f32[1536,1536]{1,0:T(8,128)}), f32[1536,1536]{1,0:T(8,128)}) %all-reduce.2.cloned.1.call-update) | async-done | bytes 9437200 | tf_op jit(solution)/shard_map/psum | solution.py:120
  335.7 7.2 %multiply_convert_fusion = bf16[1536,1536]{1,0:T(8,128)(2,1)} fusion(f32[1536,1536]{1,0:T(8,128)} %all-reduce.2.cloned.1.call-done), kind=kLoop, calls=%fused_computation.5 | loop fusion | flops 4718592 | bytes 14155776 | tf_op jit(solution)/shard_map/convert_element_type | solution.py:121
  343.0 0.0 copy-done.1
  (10 shorter events, 0.1 us)
Async XLA Ops:
  7.2 134.5 %copy-start = (bf16[768,1536]{1,0:T(8,128)(2,1)S(1)}, bf16[768,1536]{1,0:T(8,128)(2,1)}, u32[]{:S(2)}) copy-start(bf16[768,1536]{1,0:T(8,128)(2,1)} %param.16) | copy-start | bytes 7077892
  7.2 6.9 %copy-start.3 = (bf16[1,256,1536]{2,1,0:T(8,128)(2,1)S(1)}, bf16[1,256,1536]{2,1,0:T(8,128)(2,1)}, u32[]{:S(2)}) copy-start(bf16[1,256,1536]{2,1,0:T(8,128)(2,1)} %param.10) | copy-start | bytes 2359300
  7.2 51.0 %all-gather.3.cloned.1.call-start = ((), (), s32[]{:S(2)}) async-start(), calls=%async_computation | async-start | bytes 2228224 | tf_op jit(solution)/shard_map/all_gather | solution.py:55
  9.8 112.8 %all-gather.5.cloned.1.call-start = ((), (), s32[]{:S(2)}) async-start(), calls=%async_computation.1 | async-start | bytes 6684672 | tf_op jit(solution)/shard_map/all_gather | solution.py:56
  13.4 322.4 %all-reduce.2.cloned.1.call-start = ((), (), s32[]{:S(2)}) async-start(), calls=%async_computation.2 | async-start | bytes 18874368 | tf_op jit(solution)/shard_map/psum | solution.py:120
  66.4 6.0 %copy-start.2 = (f32[4,256,4096]{2,1,0:T(8,128)}, f32[4,256,4096]{2,1,0:T(8,128)S(1)}, u32[]{:S(2)}) copy-start(f32[4,256,4096]{2,1,0:T(8,128)S(1)} %get-tuple-element.17) | copy-start | bytes 50331652
  150.5 7.6 %copy-start.4 = (f32[3,1536]{1,0:T(4,128)S(1)}, f32[3,1536]{1,0:T(4,128)}, u32[]{:S(2)}) copy-start(f32[3,1536]{1,0:T(4,128)} %param.17) | copy-start | bytes 55300
  150.5 10.4 %copy-start.5 = (bf16[1,512,1536]{2,1,0:T(8,128)(2,1)S(1)}, bf16[1,512,1536]{2,1,0:T(8,128)(2,1)}, u32[]{:S(2)}) copy-start(bf16[1,512,1536]{2,1,0:T(8,128)(2,1)} %param.19) | copy-start | bytes 4718596
  153.4 4.7 %collective-permute-start = (bf16[1,1536]{1,0:T(2,128)(2,1)S(1)}, bf16[1,1536]{1,0:T(2,128)(2,1)S(1)}, u32[]{:S(2)}, u32[]{:S(2)}) collective-permute-start(bf16[1,1536]{1,0:T(2,128)(2,1)S(1)} %get-tuple-element.12), channel_id=1, source_target_pairs={{0,1},{1,2},{2,3},{3,4},{4,5},{5,6},{6,7},{7,8},{8,9},{9,10},{10,1... | collective-permute-start | bytes 9224 | tf_op jit(solution)/shard_map/ppermute | solution.py:21
  156.6 4.4 %collective-permute-start.1 = (bf16[1,1536]{1,0:T(2,128)(2,1)S(1)}, bf16[1,1536]{1,0:T(2,128)(2,1)S(1)}, u32[]{:S(2)}, u32[]{:S(2)}) collective-permute-start(bf16[1,1536]{1,0:T(2,128)(2,1)S(1)} %get-tuple-element.13), channel_id=1, source_target_pairs={{1,0},{2,1},{3,2},{4,3},{5,4},{6,5},{7,6},{8,7},{9,8},{10,9},{11,1... | collective-permute-start | bytes 9224 | tf_op jit(solution)/shard_map/ppermute | solution.py:23
  175.1 5.3 %collective-permute-start.2 = (bf16[1,1536]{1,0:T(2,128)(2,1)S(1)}, bf16[1,1536]{1,0:T(2,128)(2,1)S(1)}, u32[]{:S(2)}, u32[]{:S(2)}) collective-permute-start(bf16[1,1536]{1,0:T(2,128)(2,1)S(1)} %get-tuple-element.10), channel_id=1, source_target_pairs={{1,0},{2,1},{3,2},{4,3},{5,4},{6,5},{7,6},{8,7},{9,8},{10,9},{11,1... | collective-permute-start | bytes 9224 | tf_op jit(solution)/shard_map/ppermute | solution.py:23
  176.4 4.8 %collective-permute-start.3 = (bf16[1,1536]{1,0:T(2,128)(2,1)S(1)}, bf16[1,1536]{1,0:T(2,128)(2,1)S(1)}, u32[]{:S(2)}, u32[]{:S(2)}) collective-permute-start(bf16[1,1536]{1,0:T(2,128)(2,1)S(1)} %get-tuple-element.11), channel_id=1, source_target_pairs={{0,1},{1,2},{2,3},{3,4},{4,5},{5,6},{6,7},{7,8},{8,9},{9,10},{10,1... | collective-permute-start | bytes 9224 | tf_op jit(solution)/shard_map/ppermute | solution.py:21
  335.7 7.2 %copy-start.1 = (bf16[768,1536]{1,0:T(8,128)(2,1)S(1)}, bf16[768,1536]{1,0:T(8,128)(2,1)}, u32[]{:S(2)}) copy-start(bf16[768,1536]{1,0:T(8,128)(2,1)} %param.16) | copy-start | bytes 7077892
Sparse Core Ops, SparseCore 0:
  10.7 47.4 all-gather.2
  60.9 61.6 all-gather.4
  167.6 168.0 all-reduce.1
where the time goes:
time: 350 us
  waiting for transfers between devices  168 us (48%)
  blocking collectives  74.9 us (21%)
  matrix products  36.9 us (11%)
  local copies, waits for them, and re-layouts  26.7 us (8%)
  other arithmetic  18.4 us (5%)
  between operations  14.6 us (4%)
  starting transfers between devices  9.98 us (3%)
    psum x1, waiting for transfers between devices, local(): point_total, depth_total = lax.psum((point_term, depth_term), ('dp', 'seq'))  75.5 us
    psum x1, blocking collectives, local(): point_total, depth_total = lax.psum((point_term, depth_term), ('dp', 'seq'))  74.9 us
    all_gather x1, waiting for transfers between devices, local(): value_piece = lax.all_gather(values, 'seq', axis=0, tiled=True)  46.3 us
    all_gather x1, waiting for transfers between devices, local(): key_piece = lax.all_gather(keys, 'seq', axis=0, tiled=True)  42.6 us
    dot_general x1, matrix products, local(): jnp.einsum('hqk,khd->qhd', weights_raw.astype(jnp.bfloat16), value_heads,...  10.3 us
    all_gather x1, local copies, waits for them, and re-layouts, local(): value_piece = lax.all_gather(values, 'seq', axis=0, tiled=True)  8.63 us
    dot_general x1, matrix products, local(): lax.dot_general(upstream, point_weight, (((1,), (1,)), ((), ())), preferr...  7.54 us
    convert_element_type x1, other arithmetic, local(): grad_pointwise = (point_total * norm_scale).astype(jnp.bfloat16)  7.24 us
  transfers between devices with their start and end apart: 7, of which 5 were waited for; matrix products, arithmetic and copies ran while one was open for 8% of the time, Pallas kernels for 0%

commit v1 on v0

--- a/solution.py
+++ b/solution.py
@@ -117,7 +117,11 @@
     point_term = lax.dot_general(
         activated, upstream, (((0,), (0,)), ((), ())), preferred_element_type=jnp.float32
     )
-    point_total, depth_total = lax.psum((point_term, depth_term), ("dp", "seq"))
+
+    def connect_the_area(a0):
+        return lax.psum(lax.psum(a0, axis_name="seq"), axis_name="dp")
+
+    point_total, depth_total = connect_the_area((point_term, depth_term))
     grad_pointwise = (point_total * norm_scale).astype(jnp.bfloat16)
     return (grad_pointwise, depth_total * norm_scale, grad_skip[None])
 

time: 350 us -> 452 us (1.29)
  waiting for transfers between devices: 168 us -> 248 us
  blocking collectives: 74.9 us -> 96 us
    psum x1 -> x2, waiting for transfers between devices: 75.5 us -> 156 us  [connect_the_area(): return lax.psum(lax.psum(a0, axis_name='seq'), axis_name='dp')]
    psum x1 -> x2, blocking collectives: 74.9 us -> 96 us  [connect_the_area(): return lax.psum(lax.psum(a0, axis_name='seq'), axis_name='dp')]
  transfers between devices with their start and end apart: 7 -> 8, of which waited for: 5 -> 6; matrix products, arithmetic and copies ran while one was open for 8% -> 6% of each run, Pallas kernels for 0% -> 0%
where the time goes in v1:
time: 452 us; the launch traced here: 451 us
  waiting for transfers between devices  248 us (55%)
  blocking collectives  96 us (21%)
  matrix products  36.9 us (8%)
  local copies, waits for them, and re-layouts  26.7 us (6%)
  other arithmetic  18.4 us (4%)
  between operations  14.6 us (3%)
  starting transfers between devices  10 us (2%)
    psum x2, waiting for transfers between devices, connect_the_area(): return lax.psum(lax.psum(a0, axis_name='seq'), axis_name='dp')  156 us
    psum x2, blocking collectives, connect_the_area(): return lax.psum(lax.psum(a0, axis_name='seq'), axis_name='dp')  96 us
    all_gather x1, waiting for transfers between devices, local(): value_piece = lax.all_gather(values, 'seq', axis=0, tiled=True)  46.3 us
    all_gather x1, waiting for transfers between devices, local(): key_piece = lax.all_gather(keys, 'seq', axis=0, tiled=True)  42.6 us
    dot_general x1, matrix products, local(): jnp.einsum('hqk,khd->qhd', weights_raw.astype(jnp.bfloat16), value_heads,...  10.3 us
  transfers between devices with their start and end apart: 8, of which 6 were waited for; matrix products, arithmetic and copies ran while one was open for 6% of the time, Pallas kernels for 0%

profile of v1, /device:TPU:1, one launch (start us, length us, event | category | flops | bytes accessed | tf_op | source)
XLA Modules:
  0.0 451.0 jit_solution(2276133366466179838)
XLA Ops:
  7.2 0.0 copy-start
  7.2 0.0 copy-start.3
  7.2 0.0 all-gather.3.cloned.1.call-start
  7.2 2.6 convolution_convert_fusion.1
  9.8 0.0 all-gather.3.cloned.1.call-update
  9.8 0.0 all-gather.5.cloned.1.call-start
  9.9 3.4 convolution_convert_fusion
  13.3 0.0 all-gather.5.cloned.1.call-update
  13.4 0.0 all-reduce.3.cloned.1.call-start
  14.1 0.0 copy-done.3
  14.1 1.6 convolution_convert_fusion.2
  15.7 42.6 %all-gather.3.cloned.1.call-done = bf16[4096,256]{1,0:T(8,128)(2,1)} async-done(((bf16[256,256]{1,0:T(8,128)(2,1)}), bf16[4096,256]{1,0:T(8,128)(2,1)}) %all-gather.3.cloned.1.call-update) | async-done | bytes 2097168 | tf_op jit(solution)/shard_map/all_gather | solution.py:55
  58.2 4.1 copy.15
  62.3 4.1 fusion
  66.4 5.9 %copy-done.2 = f32[4,256,4096]{2,1,0:T(8,128)} copy-done((f32[4,256,4096]{2,1,0:T(8,128)}, f32[4,256,4096]{2,1,0:T(8,128)S(1)}, u32[]{:S(2)}) %copy-start.2) | copy-done | bytes 16777240
  72.4 4.0 fusion.1
  76.4 46.3 %all-gather.5.cloned.1.call-done = bf16[4096,768]{1,0:T(8,128)(2,1)} async-done(((bf16[256,768]{1,0:T(8,128)(2,1)}), bf16[4096,768]{1,0:T(8,128)(2,1)}) %all-gather.5.cloned.1.call-update) | async-done | bytes 6291472 | tf_op jit(solution)/shard_map/all_gather | solution.py:56
  122.7 8.6 %copy.16 = bf16[4096,768]{0,1:T(8,128)(2,1)} copy(bf16[4096,768]{1,0:T(8,128)(2,1)} %all-gather.5.cloned.1.call-done) | data formatting | bytes 12582912 | tf_op jit(solution)/shard_map/all_gather | solution.py:56
  131.3 10.3 %multiply_reduce_fusion = (f32[256]{0:T(256)S(1)}, f32[256,4,192]{0,2,1:T(8,128)S(1)}) fusion(f32[256,4]{0,1:T(4,128)S(1)} %bitcast.50, bf16[4096,4,192]{0,2,1:T(8,128)(2,1)} %bitcast.48, f32[4,256,4096]{2,1,0:T(8,128)} %copy-done.2, f32[4,256]{1,0:T(4,128)S(1)} %get-tuple-element.15, pred[4096]{0:T(1024)(128)(4,1)S(1)} %iota_compare_fusion, ...), kind=kOutput, calls=%fused_computation.68 | convolution fusion | flops 1628176128 | bytes 23872512 | tf_op jit(solution)/shard_map/hqk,khd->qhd/dot_general | solution.py:70
  141.6 0.1 fusion.51
  141.7 0.0 copy-done
  141.7 0.8 fusion.26
  142.5 2.7 broadcast_in_dim.33
  145.2 5.2 %convert_element_type.79 = f32[512,1536]{1,0:T(8,128)} reshape(f32[256,2,1536]{2,1,0:T(2,128)} %broadcast_in_dim.33) | data formatting | bytes 6291456 | tf_op jit(solution)/shard_map/convert_element_type | solution.py:87
  150.5 2.9 fusion.24
  153.4 3.1 collective-permute-start
  156.6 1.5 collective-permute-start.1
  158.0 0.0 copy-done.4
  158.0 0.1 slice_reduce_fusion.2
  158.1 0.0 collective-permute-done
  158.1 2.8 collective-permute-done.1
  160.9 0.0 copy-done.5
  160.9 6.6 %fusion.27 = f32[1536,1536]{1,0:T(8,128)} fusion(bf16[512,1536]{1,0:T(8,128)(2,1)S(1)} %fusion.24, bf16[1,1536]{1,0:T(2,128)(2,1)S(1)} %collective-permute-done.1, bf16[1,1536]{1,0:T(2,128)(2,1)S(1)} %collective-permute-done, bf16[1,512,1536]{2,1,0:T(8,128)(2,1)S(1)} %copy-done.5, f32[1536]{0:T(1024)S(1)} %get-tuple-element.7, ...), kind=kOutput, calls=%fused_computation.41 | convolution fusion | flops 2434007040 | bytes 12607488 | tf_op jit(solution)/shard_map/dot_general | solution.py:117
  167.5 0.0 all-reduce.3.cloned.1.call-update
  167.5 0.0 all-reduce.5.cloned.1.call-start
  167.6 154.1 %all-reduce.3.cloned.1.call-done = f32[1536,1536]{1,0:T(8,128)} async-done(((f32[1536,1536]{1,0:T(8,128)}), f32[1536,1536]{1,0:T(8,128)}) %all-reduce.3.cloned.1.call-update) | async-done | bytes 9437200 | tf_op jit(solution)/shard_map/psum | solution.py:122
  321.7 0.0 all-reduce.5.cloned.1.call-update
  321.7 7.5 %fusion.17 = bf16[512,1536]{1,0:T(8,128)(2,1)S(1)} fusion(bf16[1,1536]{1,0:T(2,128)(2,1)S(1)} %collective-permute-done.1, bf16[512,1536]{1,0:T(8,128)(2,1)S(1)} %fusion.24, bf16[1,1536]{1,0:T(2,128)(2,1)S(1)} %collective-permute-done, bf16[1536,1536]{1,0:T(8,128)(2,1)} %param.18, bf16[1,512,1536]{2,1,0:T(8,128)(2,1)} %param.19, ...), kind=kOutput, calls=%fused_computation.28 | convolution fusion | flops 2442657792 | bytes 9461760 | tf_op jit(solution)/shard_map/dot_general | solution.py:98
  329.3 1.3 collective-permute-start.2
  330.6 4.0 collective-permute-start.3
  334.6 0.0 collective-permute-done.2
  334.6 0.7 collective-permute-done.3
  335.3 3.5 fusion.18
  338.9 59.0 %psum.30 = f32[3,1536]{1,0:T(4,128)S(1)} all-reduce(f32[3,1536]{1,0:T(4,128)S(1)} %pad_maximum_fusion.5), channel_id=1, replica_groups=mesh['dp'=8,'seq'=16] {'seq'}, use_global_device_ids=true, to_apply=%region_8.9 | all-reduce | flops 4608 | bytes 36864 | tf_op jit(solution)/shard_map/psum | solution.py:122
  397.9 37.0 %psum.31 = f32[3,1536]{1,0:T(4,128)S(1)} all-reduce(f32[3,1536]{1,0:T(4,128)S(1)} %psum.30), channel_id=1, replica_groups=mesh['dp'=8,'seq'=16] {'dp'}, use_global_device_ids=true, to_apply=%region_9.10 | all-reduce | flops 4608 | bytes 36864 | tf_op jit(solution)/shard_map/psum | solution.py:122
  434.9 0.6 broadcast_multiply_fusion
  435.5 1.7 all-reduce.5.cloned.1.call-done
  437.2 7.2 %multiply_convert_fusion = bf16[1536,1536]{1,0:T(8,128)(2,1)} fusion(f32[1536,1536]{1,0:T(8,128)} %all-reduce.5.cloned.1.call-done), kind=kLoop, calls=%fused_computation.5 | loop fusion | flops 4718592 | bytes 14155776 | tf_op jit(solution)/shard_map/convert_element_type | solution.py:125
  (14 shorter events, 0.1 us)
Async XLA Ops:
  7.2 134.5 %copy-start = (bf16[768,1536]{1,0:T(8,128)(2,1)S(1)}, bf16[768,1536]{1,0:T(8,128)(2,1)}, u32[]{:S(2)}) copy-start(bf16[768,1536]{1,0:T(8,128)(2,1)} %param.16) | copy-start | bytes 7077892
  7.2 6.9 %copy-start.3 = (bf16[1,256,1536]{2,1,0:T(8,128)(2,1)S(1)}, bf16[1,256,1536]{2,1,0:T(8,128)(2,1)}, u32[]{:S(2)}) copy-start(bf16[1,256,1536]{2,1,0:T(8,128)(2,1)} %param.10) | copy-start | bytes 2359300
  7.2 51.0 %all-gather.3.cloned.1.call-start = ((), (), s32[]{:S(2)}) async-start(), calls=%async_computation | async-start | bytes 2228224 | tf_op jit(solution)/shard_map/all_gather | solution.py:55
  9.8 112.8 %all-gather.5.cloned.1.call-start = ((), (), s32[]{:S(2)}) async-start(), calls=%async_computation.1 | async-start | bytes 6684672 | tf_op jit(solution)/shard_map/all_gather | solution.py:56
  13.4 308.3 %all-reduce.3.cloned.1.call-start = ((), (), s32[]{:S(2)}) async-start(), calls=%async_computation.2 | async-start | bytes 18874368 | tf_op jit(solution)/shard_map/psum | solution.py:122
  66.4 6.0 %copy-start.2 = (f32[4,256,4096]{2,1,0:T(8,128)}, f32[4,256,4096]{2,1,0:T(8,128)S(1)}, u32[]{:S(2)}) copy-start(f32[4,256,4096]{2,1,0:T(8,128)S(1)} %get-tuple-element.17) | copy-start | bytes 50331652
  150.5 7.6 %copy-start.4 = (f32[3,1536]{1,0:T(4,128)S(1)}, f32[3,1536]{1,0:T(4,128)}, u32[]{:S(2)}) copy-start(f32[3,1536]{1,0:T(4,128)} %param.17) | copy-start | bytes 55300
  150.5 10.4 %copy-start.5 = (bf16[1,512,1536]{2,1,0:T(8,128)(2,1)S(1)}, bf16[1,512,1536]{2,1,0:T(8,128)(2,1)}, u32[]{:S(2)}) copy-start(bf16[1,512,1536]{2,1,0:T(8,128)(2,1)} %param.19) | copy-start | bytes 4718596
  153.4 4.7 %collective-permute-start = (bf16[1,1536]{1,0:T(2,128)(2,1)S(1)}, bf16[1,1536]{1,0:T(2,128)(2,1)S(1)}, u32[]{:S(2)}, u32[]{:S(2)}) collective-permute-start(bf16[1,1536]{1,0:T(2,128)(2,1)S(1)} %get-tuple-element.12), channel_id=1, source_target_pairs={{0,1},{1,2},{2,3},{3,4},{4,5},{5,6},{6,7},{7,8},{8,9},{9,10},{10,1... | collective-permute-start | bytes 9224 | tf_op jit(solution)/shard_map/ppermute | solution.py:21
  156.6 4.4 collective-permute-start.1
  167.5 269.7 %all-reduce.5.cloned.1.call-start = ((), (), s32[]{:S(2)}) async-start(), calls=%async_computation.3 | async-start | bytes 18874368 | tf_op jit(solution)/shard_map/psum | solution.py:122
  329.3 5.3 %collective-permute-start.2 = (bf16[1,1536]{1,0:T(2,128)(2,1)S(1)}, bf16[1,1536]{1,0:T(2,128)(2,1)S(1)}, u32[]{:S(2)}, u32[]{:S(2)}) collective-permute-start(bf16[1,1536]{1,0:T(2,128)(2,1)S(1)} %get-tuple-element.10), channel_id=1, source_target_pairs={{1,0},{2,1},{3,2},{4,3},{5,4},{6,5},{7,6},{8,7},{9,8},{10,9},{11,1... | collective-permute-start | bytes 9224 | tf_op jit(solution)/shard_map/ppermute | solution.py:23
  330.6 4.8 %collective-permute-start.3 = (bf16[1,1536]{1,0:T(2,128)(2,1)S(1)}, bf16[1,1536]{1,0:T(2,128)(2,1)S(1)}, u32[]{:S(2)}, u32[]{:S(2)}) collective-permute-start(bf16[1,1536]{1,0:T(2,128)(2,1)S(1)} %get-tuple-element.11), channel_id=1, source_target_pairs={{0,1},{1,2},{2,3},{3,4},{4,5},{5,6},{6,7},{7,8},{8,9},{9,10},{10,1... | collective-permute-start | bytes 9224 | tf_op jit(solution)/shard_map/ppermute | solution.py:21
  437.2 7.2 %copy-start.1 = (bf16[768,1536]{1,0:T(8,128)(2,1)S(1)}, bf16[768,1536]{1,0:T(8,128)(2,1)}, u32[]{:S(2)}) copy-start(bf16[768,1536]{1,0:T(8,128)(2,1)} %param.16) | copy-start | bytes 7077892
Sparse Core Ops, SparseCore 0:
  10.7 47.4 all-gather.2
  60.9 61.6 all-gather.4
  167.6 154.0 all-reduce.2
  324.0 113.1 all-reduce.4
